TPU v7x, 256 devices: a whole 4x4x8 slice. The times are simulated.
256 devices in a mesh: row: 16 (over z_hi, y), col: 4 (over z_lo, core), depth: 4 (over x).
Axes of the slice: x: 4, y: 4, z: 8 (z_hi: 4, z_lo: 2; z = z_hi * 2 + z_lo), core: 2. Of those that a mesh axis runs over, the one named last changes fastest.
Arguments:
- integrals: float32 [32768, 4096], P(('row', 'col'), 'depth'), may hold values from -0.09375 to 0.09375
- amplitudes: float32 [4096, 64, 64], P('depth', 'col', 'row'), may hold values from -6 to 6
Outputs:
- relaid: float32 [64, 64, 32768], P(('col', 'depth'), 'row')
All inputs are finite; a program needn't handle non-finite values.
Results may differ from a plain program's by a relative error of at most 0.00007.
Values sent between devices are 32-bit elements; how exact they have to be, the bound alone decides.
No kernel may reach another device: no remote copies, remote signals or barrier semaphores. Data moves between devices by JAX's collectives and lax.ppermute only.
A program may use at most 64 MiB of HBM per device.

v0:
```python
import jax
import jax.numpy as jnp
from jax import lax
from jax.sharding import PartitionSpec as P


def shards(integrals, amplitudes):
    rows_w = lax.all_gather(integrals, "col", axis=0, tiled=True)
    panel_t = lax.all_gather(amplitudes, "row", axis=2, tiled=True)
    kc_rows, i_count, j_count = panel_t.shape
    flat_panel = panel_t.reshape(kc_rows, i_count * j_count)
    row_count = lax.axis_size("row")
    ab_rows = rows_w.shape[0]
    summed = lax.psum_scatter(
        lax.dot_general(
            flat_panel,
            rows_w,
            (((0,), (1,)), ((), ())),
            precision=lax.Precision.HIGHEST,
            preferred_element_type=jnp.float32,
        ),
        "depth",
        scatter_dimension=0,
        tiled=True,
    )
    shares = summed.reshape(-1, j_count // row_count, row_count, ab_rows)
    exchanged = lax.all_to_all(shares, "row", split_axis=2, concat_axis=3, tiled=True)
    result = exchanged.reshape(shares.shape[0], j_count // row_count, row_count * ab_rows)
    return result


def solution(mesh):
    placed = (P(("row", "col"), "depth"), P("depth", "col", "row"))
    return jax.shard_map(
        shards,
        mesh=mesh,
        in_specs=placed,
        out_specs=P(("col", "depth"), "row", None),
        check_vma=False,
    )
```

profile of v0, /device:TPU:1, one launch (start us, length us, event | category | flops | bytes accessed | tf_op | source)
XLA Modules:
  0.0 360.2 jit_solution(4689598038092722052)
XLA Ops:
  6.5 0.0 all-gather.3.cloned.1.call-start
  6.5 1.8 copy.5
  8.3 0.0 all-gather.3.cloned.1.call-update
  8.4 0.0 all-gather.5.cloned.1.call-start
  8.4 0.7 all-gather.5.cloned.1.call-update
  9.1 0.0 reduce-scatter.2.cloned.1.call-start
  9.2 79.2 %all-gather.3.cloned.1.call-done = f32[1024,16,64]{0,1,2:T(8,128)} async-done(((f32[1024,16,4]{0,1,2:T(8,128)}), f32[1024,16,64]{0,1,2:T(8,128)}) %all-gather.3.cloned.1.call-update) | async-done | bytes 4194320 | tf_op jit(solution)/shard_map/all_gather | solution.py:9
  88.3 6.6 %copy.6 = f32[1024,16,64]{0,2,1:T(8,128)} copy(f32[1024,16,64]{0,1,2:T(8,128)} %all-gather.3.cloned.1.call-done) | data formatting | bytes 8388608 | tf_op jit(solution)/shard_map/all_gather | solution.py:9
  94.9 80.8 %all-gather.5.cloned.1.call-done = f32[2048,1024]{1,0:T(8,128)} async-done(((f32[512,1024]{1,0:T(8,128)}), f32[2048,1024]{1,0:T(8,128)}) %all-gather.5.cloned.1.call-update) | async-done | bytes 8388624 | tf_op jit(solution)/shard_map/all_gather | solution.py:8
  175.7 31.0 %fusion = f32[1024,2048]{1,0:T(8,128)} fusion(f32[1024,1024]{0,1:T(8,128)} %bitcast.7, f32[2048,1024]{1,0:T(8,128)} %all-gather.5.cloned.1.call-done), kind=kOutput, calls=%fused_computation | convolution fusion | flops 25769803776 | bytes 20971520 | tf_op jit(solution)/shard_map/dot_general | solution.py:15
  206.6 0.0 reduce-scatter.2.cloned.1.call-update
  206.7 83.1 %reduce-scatter.2.cloned.1.call-done = f32[256,2048]{1,0:T(8,128)} async-done(((f32[1024,2048]{1,0:T(8,128)}), f32[256,2048]{1,0:T(8,128)}) %reduce-scatter.2.cloned.1.call-update) | async-done | bytes 2097168 | tf_op jit(solution)/shard_map/reduce_scatter | solution.py:14
  289.8 2.9 copy.7
  292.7 59.5 %all_to_all.4 = f32[4,4,16,2048]{3,1,0,2:T(4,128)S(1)} all-to-all(f32[4,4,16,2048]{3,1,0,2:T(4,128)S(1)} %copy.7), channel_id=1, replica_groups=mesh['row'=16,'col'=4,'depth'=4] {'row'}, dimensions={2} | all-to-all | bytes 4194304 | tf_op jit(solution)/shard_map/all_to_all | solution.py:27
  352.3 1.5 copy.9
Async XLA Ops:
  6.5 81.8 %all-gather.3.cloned.1.call-start = ((), (), s32[]{:S(2)}) async-start(), calls=%async_computation.2 | async-start | bytes 4456448 | tf_op jit(solution)/shard_map/all_gather | solution.py:9
  8.4 167.3 %all-gather.5.cloned.1.call-start = ((), (), s32[]{:S(2)}) async-start(), calls=%async_computation.3 | async-start | bytes 10485760 | tf_op jit(solution)/shard_map/all_gather | solution.py:8
  9.1 280.7 %reduce-scatter.2.cloned.1.call-start = ((), (), s32[]{:S(2)}) async-start(), calls=%async_computation.4 | async-start | bytes 10485760 | tf_op jit(solution)/shard_map/reduce_scatter | solution.py:14
Sparse Core Ops, SparseCore 0:
  9.8 78.4 all-gather.2
  90.1 85.4 all-gather.4
  206.8 82.9 reduce-scatter.1
where the time goes:
time: 360 us
  waiting for transfers between devices  244 us (68%)
  blocking collectives  59.5 us (17%)
  matrix products  31 us (9%)
  between operations  13.1 us (4%)
  local copies, waits for them, and re-layouts  12.8 us (4%)
    reduce_scatter x1, waiting for transfers between devices, shards(): lax.psum_scatter(lax.dot_general(flat_panel, rows_w, (((0,), (1,)), ((),...  83.1 us
    all_gather x1, waiting for transfers between devices, shards(): rows_w = lax.all_gather(integrals, 'col', axis=0, tiled=True)  80.8 us
    all_gather x1, waiting for transfers between devices, shards(): panel_t = lax.all_gather(amplitudes, 'row', axis=2, tiled=True)  79.2 us
    all_to_all x1, blocking collectives, shards(): lax.all_to_all(shares, 'row', split_axis=2, concat_axis=3, tiled=True)  59.5 us
    dot_general x1, matrix products, shards(): lax.dot_general(flat_panel, rows_w, (((0,), (1,)), ((), ())), precision=l...  31 us
  transfers between devices with their start and end apart: 3, of which 3 were waited for; matrix products, arithmetic and copies ran while one was open for 2% of the time, Pallas kernels for 0%

commit v1 on v0

v1 whole, which is shorter than its diff:
```python
import functools

import jax
import jax.numpy as jnp
import numpy as np
from jax import lax
from jax.experimental import pallas as pl
from jax.experimental.pallas import tpu as pltpu
from jax.sharding import Mesh
from jax.sharding import PartitionSpec as P

AXES = ("zh", "y", "zl", "c", "x")
SIZES = (4, 4, 2, 2, 4)
VMEM = 48 * 2**20
F32, BF16 = jnp.float32, jnp.bfloat16


def move(value, y=0, z=0, c=0):
    pairs = []
    for source, (at_zh, at_y, at_zl, at_c, at_x) in enumerate(np.ndindex(*SIZES)):
        to_z = (2 * at_zh + at_zl + z) % 8
        to = (to_z // 2, (at_y + y) % 4, to_z % 2, (at_c + c) % 2, at_x)
        pairs.append((source, int(np.ravel_multi_index(to, SIZES))))
    return lax.ppermute(value, AXES, pairs)


def split(value):
    high = value.astype(BF16)
    return high, (value - high.astype(F32)).astype(BF16)


def product(t_high, t_low, w):
    w_high, w_low = split(w)
    dot = functools.partial(lax.dot_general, dimension_numbers=(((1,), (1,)), ((), ())), preferred_element_type=F32)
    return dot(t_high, w_high) + (dot(t_high, w_low) + dot(t_low, w_high))


def first_kernel(place, s0, s1, s2, s3, w0, w1, out, t_high, t_low, t):
    step = pl.program_id(0)

    @pl.when(step == 0)
    def _():
        for d, shard in enumerate((s0, s1, s2, s3)):
            at = lax.rem(place[0] + d, 4)
            for x in range(4):
                for j in range(4):
                    t[x, at, 4 * j : 4 * j + 4, :] = shard[4 * x : 4 * x + 4, j, :]
        high, low = split(t[...].reshape(256, -1))
        t_high[...] = high
        t_low[...] = low

    def work(w):
        out[...] = product(t_high[...], t_low[...], w[...]).reshape(out.shape)

    pl.when(step < 2)(lambda: work(w0))
    pl.when(step >= 2)(lambda: work(w1))


def first(place, parts, w0, w1):
    kc = w0.shape[1]
    whole = pl.BlockSpec((16, 4, kc), lambda s: (0, 0, 0))
    return pl.pallas_call(
        first_kernel,
        grid=(4,),
        in_specs=[
            pl.BlockSpec(memory_space=pltpu.SMEM),
            *[whole] * 4,
            pl.BlockSpec((256, kc), lambda s: (jnp.minimum(s, 1), 0)),
            pl.BlockSpec((256, kc), lambda s: (jnp.maximum(s - 2, 0), 0)),
        ],
        out_specs=[
            pl.BlockSpec((4, 64, 256), lambda s: (0, 0, s)),
            pl.BlockSpec((256, kc), lambda s: (0, 0)),
            pl.BlockSpec((256, kc), lambda s: (0, 0)),
        ],
        out_shape=[
            jax.ShapeDtypeStruct((4, 64, 1024), F32),
            jax.ShapeDtypeStruct((256, kc), BF16),
            jax.ShapeDtypeStruct((256, kc), BF16),
        ],
        scratch_shapes=[pltpu.VMEM((4, 4, 16, kc), F32)],
        compiler_params=pltpu.CompilerParams(vmem_limit_bytes=VMEM),
        cost_estimate=pl.CostEstimate(flops=6 * 256 * 1024 * kc, bytes_accessed=10 * 2**20, transcendentals=0),
    )(place, *parts, w0, w1)


def second_kernel(*refs):
    groups, (w0, w1, out) = refs[:8], refs[8:]

    def work(w):
        for d in range(4):
            block = product(groups[2 * d][...], groups[2 * d + 1][...], w[...])
            out[:, :, 4 * d : 4 * d + 4, :] = block.reshape(4, 16, 4, -1)

    step = pl.program_id(0)
    pl.when(step < 1)(lambda: work(w0))
    pl.when(step >= 1)(lambda: work(w1))


def second(groups, w0, w1):
    kc = w0.shape[1]
    pair = pl.BlockSpec((256, kc), lambda s: (0, 0))
    return pl.pallas_call(
        second_kernel,
        grid=(2,),
        in_specs=[pair] * 10,
        out_specs=pl.BlockSpec((4, 16, 16, 256), lambda s: (0, 0, 0, s)),
        out_shape=jax.ShapeDtypeStruct((4, 16, 16, 512), F32),
        compiler_params=pltpu.CompilerParams(vmem_limit_bytes=VMEM),
        cost_estimate=pl.CostEstimate(flops=6 * 1024 * 512 * kc, bytes_accessed=9 * 2**20, transcendentals=0),
    )(*[g for pair in groups for g in pair], w0, w1)


def place_kernel(place, part, *rest):
    out = rest[-1]
    at = pl.program_id(0) // 4
    for d in range(4):
        t = lax.rem(at + d, 4)
        for i in range(4):
            out[i, pl.ds(t, 1), :] = part[0, 4 * d + i : 4 * d + i + 1, :]


def placed(place, part, width, column, out=None):
    n = part.shape[2] // width
    return pl.pallas_call(
        place_kernel,
        grid_spec=pltpu.PrefetchScalarGridSpec(
            num_scalar_prefetch=1,
            grid=(16, n),
            in_specs=[pl.BlockSpec((1, 16, width), lambda s, q, p: (s, 0, q))]
            + ([] if out is None else [pl.BlockSpec(memory_space=pl.ANY)]),
            out_specs=pl.BlockSpec((4, 4, width), lambda s, q, p: (0, 0, column(s, q, p))),
        ),
        out_shape=jax.ShapeDtypeStruct((4, 4, 32768), F32),
        input_output_aliases={} if out is None else {2: 0},
        compiler_params=pltpu.CompilerParams(vmem_limit_bytes=VMEM),
        cost_estimate=pl.CostEstimate(flops=0, bytes_accessed=8 * part.size, transcendentals=0),
    )(place, part, *([] if out is None else [out]))


def own_column(s, q, p):
    return s * 4 + p[1] * 2 + lax.rem(p[2] + q, 2)


def next_column(step, half):
    def column(s, q, p):
        z = lax.rem(2 * (s // 4) + p[1] + step + 8, 8)
        return 2 * (((z // 2) * 4 + lax.rem(s, 4)) * 4 + lax.rem(z, 2) * 2 + lax.rem(p[2] + q, 2)) + half

    return column


def shards(integrals, amplitudes):
    place = jnp.stack([lax.axis_index(n).astype(jnp.int32) for n in ("y", "zl", "c")])
    t0 = jnp.transpose(amplitudes, (1, 2, 0))

    def along_y(t):
        return t, move(t, y=-1), move(t, y=2), move(t, y=1)

    w1 = move(integrals, c=1)
    near = [along_y(t0)]
    t1, t3 = move(t0, z=-2), move(t0, z=2)
    t2 = move(t0, z=4)
    up, down = move(integrals[256:], z=1), move(integrals[:256], z=-1)
    up1, down1 = move(up, c=1), move(down, c=1)
    near += [along_y(t) for t in (t1, t2, t3)]

    def summed(part):
        return lax.psum_scatter(part, "x", scatter_dimension=0)

    sums, groups = [], [None] * 4
    for d in (0, 1, 3, 2):
        part, *groups[d] = first(place, near[d], integrals, w1)
        sums.append((d, summed(part)))
    sums = [s.reshape(16, 4, 1024) for _, s in sorted(sums, key=lambda pair: pair[0])]

    def relaid(value):
        return lax.all_to_all(value, ("zh", "y"), split_axis=0, concat_axis=0, tiled=True)

    own = relaid(jnp.concatenate(sums, axis=1))
    third = relaid(summed(second(groups, down, down1)))
    fourth = relaid(summed(second(groups, up, up1)))
    out = placed(place, own, 512, own_column)
    out = placed(place, third, 256, next_column(1, 0), out)
    return placed(place, fourth, 256, next_column(-1, 1), out)


def solution(mesh):
    fine = Mesh(mesh.devices.reshape(SIZES), AXES)
    return jax.shard_map(
        shards,
        mesh=fine,
        in_specs=(P(("zh", "y", "zl", "c"), "x"), P("x", ("zl", "c"), ("zh", "y"))),
        out_specs=P(("zl", "c", "x"), ("zh", "y"), None),
        check_vma=False,
    )
```

time: 360 us -> 325 us (0.903); the launches traced: 360 us -> 321 us
  waiting for transfers between devices: 244 us -> 132 us
  Pallas kernels: 0 us -> 67.9 us
  starting transfers between devices: 0.08 us -> 45.6 us
  matrix products: 31 us -> 0 us
  blocking collectives: 59.5 us -> 35 us
  local copies, waits for them, and re-layouts: 12.8 us -> 27.3 us
    all_gather x2 -> x0, waiting for transfers between devices: 160 us -> none  [the longest x1 80.8 us: shards(): rows_w = lax.all_gather(integrals, 'col', axis=0, tiled=True)]
    ppermute x0 -> x20, waiting for transfers between devices: none -> 117 us  [move(): return lax.ppermute(value, AXES, pairs)]
    reduce_scatter x1 -> x6, waiting for transfers between devices: 83.1 us -> 0.11 us  [summed(): return lax.psum_scatter(part, 'x', scatter_dimension=0)]
    pallas_call x0 -> x9, Pallas kernels: none -> 67.9 us  [the longest x3 32.6 us: placed(): pl.pallas_call(place_kernel, grid_spec=pltpu.PrefetchScalarGridSpec(num_s...]
    ppermute x0 -> x20, starting transfers between devices: none -> 34.1 us  [move(): return lax.ppermute(value, AXES, pairs)]
    dot_general x1 -> x0, matrix products: 31 us -> none  [shards(): lax.dot_general(flat_panel, rows_w, (((0,), (1,)), ((), ())), precision=l...]
    all_to_all x1, blocking collectives: 59.5 us -> 35 us  [relaid(): lax.all_to_all(value, ('zh', 'y'), split_axis=0, concat_axis=0, tiled=True)]
    unnamed x1 -> x58, local copies, waits for them, and re-layouts: 1.81 us -> 21.8 us
  transfers between devices with their start and end apart: 3 -> 28, of which waited for: 3 -> 19; matrix products, arithmetic and copies ran while one was open for 2% -> 2% of each run, Pallas kernels for 0% -> 16%
where the time goes in v1:
time: 325 us; the launch traced here: 321 us
  waiting for transfers between devices  132 us (41%)
  Pallas kernels  67.9 us (21%)
  starting transfers between devices  45.6 us (14%)
  blocking collectives  35 us (11%)
  local copies, waits for them, and re-layouts  27.3 us (8%)
  between operations  13.6 us (4%)
    ppermute x20, waiting for transfers between devices, move(): return lax.ppermute(value, AXES, pairs)  117 us
    all_to_all x1, blocking collectives, relaid(): lax.all_to_all(value, ('zh', 'y'), split_axis=0, concat_axis=0, tiled=True)  35 us
    ppermute x20, starting transfers between devices, move(): return lax.ppermute(value, AXES, pairs)  34.1 us
    pallas_call x3, Pallas kernels, placed(): pl.pallas_call(place_kernel, grid_spec=pltpu.PrefetchScalarGridSpec(num_s...  32.6 us
    pallas_call x4, Pallas kernels, first(): pl.pallas_call(first_kernel, grid=(4,), in_specs=[pl.BlockSpec(memory_spa...  23.1 us
    unnamed x58, local copies, waits for them, and re-layouts  21.8 us
    all_to_all x2, waiting for transfers between devices, relaid(): lax.all_to_all(value, ('zh', 'y'), split_axis=0, concat_axis=0, tiled=True)  14.1 us
    pallas_call x2, Pallas kernels, second(): pl.pallas_call(second_kernel, grid=(2,), in_specs=[pair] * 10, out_specs=...  12.1 us
  transfers between devices with their start and end apart: 28, of which 19 were waited for; matrix products, arithmetic and copies ran while one was open for 2% of the time, Pallas kernels for 16%

profile of v1, /device:TPU:1, one launch (start us, length us, event | category | flops | bytes accessed | tf_op | source)
XLA Modules:
  0.0 321.5 jit_solution(13673171001213452464)
XLA Ops:
  6.5 3.2 %collective-permute-start.3 = (f32[512,1024]{1,0:T(8,128)}, f32[512,1024]{1,0:T(8,128)}, u32[]{:S(2)}, u32[]{:S(2)}) collective-permute-start(f32[512,1024]{1,0:T(8,128)} %w0.7), channel_id=1, source_target_pairs={{0,4},{1,5},{2,6},{3,7},{4,0},{5,1},{6,2},{7,3},{8,12},{9,13},{10,... | collective-permute-start | bytes 6291464 | tf_op jit(solution)/shard_map/ppermute | solution.py:24
  9.8 4.3 %collective-permute-start.4 = (f32[16,4,1024]{2,1,0:T(4,128)}, f32[16,4,1024]{2,1,0:T(4,128)S(1)}, u32[]{:S(2)}, u32[]{:S(2)}) collective-permute-start(f32[16,4,1024]{2,1,0:T(4,128)} %bitcast.6), channel_id=1, source_target_pairs={{0,192},{1,193},{2,194},{3,195},{4,196},{5,197},{6,198},{7,199},{8... | collective-permute-start | bytes 786440 | tf_op jit(solution)/shard_map/ppermute | solution.py:24
  14.1 10.4 %collective-permute-done.4.s0 = f32[16,4,1024]{2,1,0:T(4,128)S(1)} collective-permute-done((f32[16,4,1024]{2,1,0:T(4,128)}, f32[16,4,1024]{2,1,0:T(4,128)S(1)}, u32[]{:S(2)}, u32[]{:S(2)}) %collective-permute-start.4) | collective-permute-done | bytes 262176 | tf_op jit(solution)/shard_map/ppermute | solution.py:24
  24.5 3.8 %collective-permute-start.5 = (f32[16,4,1024]{2,1,0:T(4,128)S(1)}, f32[16,4,1024]{2,1,0:T(4,128)S(1)}, u32[]{:S(2)}, u32[]{:S(2)}) collective-permute-start(f32[16,4,1024]{2,1,0:T(4,128)S(1)} %collective-permute-done.4.s0), channel_id=1, source_target_pairs={{0,48},{1,49},{2,50},{3,51},{4,52},{5,53},{6,54},{7,55},{8,56},{9,... | collective-permute-start | bytes 786440 | tf_op jit(solution)/shard_map/ppermute | solution.py:24
  29.5 4.4 %collective-permute-done.5.s1 = f32[16,4,1024]{2,1,0:T(4,128)S(1)} collective-permute-done((f32[16,4,1024]{2,1,0:T(4,128)S(1)}, f32[16,4,1024]{2,1,0:T(4,128)S(1)}, u32[]{:S(2)}, u32[]{:S(2)}) %collective-permute-start.5) | collective-permute-done | bytes 262176 | tf_op jit(solution)/shard_map/ppermute | solution.py:24
  36.5 7.2 %collective-permute-done.7.s3 = f32[16,4,1024]{2,1,0:T(4,128)S(1)} collective-permute-done((f32[16,4,1024]{2,1,0:T(4,128)S(1)}, f32[16,4,1024]{2,1,0:T(4,128)S(1)}, u32[]{:S(2)}, u32[]{:S(2)}) %collective-permute-start.7) | collective-permute-done | bytes 262176 | tf_op jit(solution)/shard_map/ppermute | solution.py:24
  45.3 5.9 %shard_map.29 = (f32[4,64,1024]{2,1,0:T(8,128)}, bf16[256,1024]{1,0:T(8,128)(2,1)S(1)}, bf16[256,1024]{1,0:T(8,128)(2,1)S(1)}) custom-call(s32[3]{0:T(128)S(1)} %pad_add_fusion.place, f32[16,4,1024]{2,1,0:T(4,128)S(1)} %collective-permute-done.4.s0, f32[16,4,1024]{2,1,0:T(4,128)S(1)} %collective-permute-done.5.s1, ...), custom_call_target="tpu_custom_call" | custom-call | flops 1610612736 | bytes 10485760 | tf_op jit(solution)/shard_map/pallas_call | solution.py:62
  52.9 3.4 %collective-permute-start.8 = (f32[16,4,1024]{2,1,0:T(4,128)S(1)}, f32[16,4,1024]{2,1,0:T(4,128)S(1)}, u32[]{:S(2)}, u32[]{:S(2)}) collective-permute-start(f32[16,4,1024]{2,1,0:T(4,128)S(1)} %bitcast.7), channel_id=1, source_target_pairs={{0,128},{1,129},{2,130},{3,131},{4,132},{5,133},{6,134},{7,135},{8... | collective-permute-start | bytes 786440 | tf_op jit(solution)/shard_map/ppermute | solution.py:24
  56.3 8.0 %collective-permute-done.8.s0 = f32[16,4,1024]{2,1,0:T(4,128)S(1)} collective-permute-done((f32[16,4,1024]{2,1,0:T(4,128)S(1)}, f32[16,4,1024]{2,1,0:T(4,128)S(1)}, u32[]{:S(2)}, u32[]{:S(2)}) %collective-permute-start.8) | collective-permute-done | bytes 262176 | tf_op jit(solution)/shard_map/ppermute | solution.py:24
  64.7 2.7 collective-permute-start.9
  67.4 4.9 %collective-permute-done.10.s2 = f32[16,4,1024]{2,1,0:T(4,128)S(1)} collective-permute-done((f32[16,4,1024]{2,1,0:T(4,128)S(1)}, f32[16,4,1024]{2,1,0:T(4,128)S(1)}, u32[]{:S(2)}, u32[]{:S(2)}) %collective-permute-start.10) | collective-permute-done | bytes 262176 | tf_op jit(solution)/shard_map/ppermute | solution.py:24
  72.3 7.4 %collective-permute-done.11.s3 = f32[16,4,1024]{2,1,0:T(4,128)S(1)} collective-permute-done((f32[16,4,1024]{2,1,0:T(4,128)S(1)}, f32[16,4,1024]{2,1,0:T(4,128)S(1)}, u32[]{:S(2)}, u32[]{:S(2)}) %collective-permute-start.11) | collective-permute-done | bytes 262176 | tf_op jit(solution)/shard_map/ppermute | solution.py:24
  79.7 5.7 %shard_map.30 = (f32[4,64,1024]{2,1,0:T(8,128)}, bf16[256,1024]{1,0:T(8,128)(2,1)S(1)}, bf16[256,1024]{1,0:T(8,128)(2,1)S(1)}) custom-call(s32[3]{0:T(128)S(1)} %pad_add_fusion.place, f32[16,4,1024]{2,1,0:T(4,128)S(1)} %collective-permute-done.8.s0, f32[16,4,1024]{2,1,0:T(4,128)S(1)} %collective-permute-done.9.s1, ...), custom_call_target="tpu_custom_call" | custom-call | flops 1610612736 | bytes 10485760 | tf_op jit(solution)/shard_map/pallas_call | solution.py:62
  86.3 8.6 %collective-permute-start.12 = (f32[16,4,1024]{2,1,0:T(4,128)S(1)}, f32[16,4,1024]{2,1,0:T(4,128)S(1)}, u32[]{:S(2)}, u32[]{:S(2)}) collective-permute-start(f32[16,4,1024]{2,1,0:T(4,128)S(1)} %bitcast.8), channel_id=1, source_target_pairs={{0,64},{1,65},{2,66},{3,67},{4,68},{5,69},{6,70},{7,71},{8,72},{9,... | collective-permute-start | bytes 786440 | tf_op jit(solution)/shard_map/ppermute | solution.py:24
  94.9 12.2 %collective-permute-done.12.s0 = f32[16,4,1024]{2,1,0:T(4,128)S(1)} collective-permute-done((f32[16,4,1024]{2,1,0:T(4,128)S(1)}, f32[16,4,1024]{2,1,0:T(4,128)S(1)}, u32[]{:S(2)}, u32[]{:S(2)}) %collective-permute-start.12) | collective-permute-done | bytes 262176 | tf_op jit(solution)/shard_map/ppermute | solution.py:24
  108.6 6.1 %collective-permute-done.13.s1 = f32[16,4,1024]{2,1,0:T(4,128)S(1)} collective-permute-done((f32[16,4,1024]{2,1,0:T(4,128)S(1)}, f32[16,4,1024]{2,1,0:T(4,128)S(1)}, u32[]{:S(2)}, u32[]{:S(2)}) %collective-permute-start.13) | collective-permute-done | bytes 262176 | tf_op jit(solution)/shard_map/ppermute | solution.py:24
  116.1 6.4 %collective-permute-done.15.s3 = f32[16,4,1024]{2,1,0:T(4,128)S(1)} collective-permute-done((f32[16,4,1024]{2,1,0:T(4,128)S(1)}, f32[16,4,1024]{2,1,0:T(4,128)S(1)}, u32[]{:S(2)}, u32[]{:S(2)}) %collective-permute-start.15) | collective-permute-done | bytes 262176 | tf_op jit(solution)/shard_map/ppermute | solution.py:24
  122.5 5.7 %shard_map.31 = (f32[4,64,1024]{2,1,0:T(8,128)}, bf16[256,1024]{1,0:T(8,128)(2,1)S(1)}, bf16[256,1024]{1,0:T(8,128)(2,1)S(1)}) custom-call(s32[3]{0:T(128)S(1)} %pad_add_fusion.place, f32[16,4,1024]{2,1,0:T(4,128)S(1)} %collective-permute-done.12.s0, f32[16,4,1024]{2,1,0:T(4,128)S(1)} %collective-permute-done.13.s1, ...), custom_call_target="tpu_custom_call" | custom-call | flops 1610612736 | bytes 10485760 | tf_op jit(solution)/shard_map/pallas_call | solution.py:62
  132.9 4.4 %collective-permute-done.s1 = f32[16,4,1024]{2,1,0:T(4,128)S(1)} collective-permute-done((f32[16,4,1024]{2,1,0:T(4,128)S(1)}, f32[16,4,1024]{2,1,0:T(4,128)S(1)}, u32[]{:S(2)}, u32[]{:S(2)}) %collective-permute-start) | collective-permute-done | bytes 262176 | tf_op jit(solution)/shard_map/ppermute | solution.py:24
  137.9 7.6 %collective-permute-done.2.s3 = f32[16,4,1024]{2,1,0:T(4,128)S(1)} collective-permute-done((f32[16,4,1024]{2,1,0:T(4,128)S(1)}, f32[16,4,1024]{2,1,0:T(4,128)S(1)}, u32[]{:S(2)}, u32[]{:S(2)}) %collective-permute-start.2) | collective-permute-done | bytes 262176 | tf_op jit(solution)/shard_map/ppermute | solution.py:24
  145.4 5.8 %shard_map.28 = (f32[4,64,1024]{2,1,0:T(8,128)}, bf16[256,1024]{1,0:T(8,128)(2,1)S(1)}, bf16[256,1024]{1,0:T(8,128)(2,1)S(1)}) custom-call(s32[3]{0:T(128)S(1)} %pad_add_fusion.place, f32[16,4,1024]{2,1,0:T(4,128)S(1)} %bitcast.12, f32[16,4,1024]{2,1,0:T(4,128)S(1)} %collective-permute-done.s1, f32[16,4,1024]{2,1,0:T(4,128)S(1)} %collective-permute-done.1.s2, ...), custom_call_target="tpu_custom_call" | custom-call | flops 1610612736 | bytes 10485760 | tf_op jit(solution)/shard_map/pallas_call | solution.py:62
  152.8 3.8 %collective-permute-done.18.refs_8_ = f32[256,1024]{1,0:T(8,128)S(1)} collective-permute-done((f32[256,1024]{1,0:T(8,128)}, f32[256,1024]{1,0:T(8,128)S(1)}, u32[]{:S(2)}, u32[]{:S(2)}) %collective-permute-start.18) | collective-permute-done | bytes 1048608 | tf_op jit(solution)/shard_map/ppermute | solution.py:24
  170.3 6.1 %shard_map.33 = f32[4,16,16,512]{3,2,1,0:T(8,128)} custom-call(bf16[256,1024]{1,0:T(8,128)(2,1)S(1)} %copy-done.22, bf16[256,1024]{1,0:T(8,128)(2,1)S(1)} %copy-done.25, bf16[256,1024]{1,0:T(8,128)(2,1)S(1)} %copy-done.4, bf16[256,1024]{1,0:T(8,128)(2,1)S(1)} %copy-done.7, bf16[256,1024]{1,0:T(8,128)(2,1)S(1)} %copy-done.10, ...), custom_call_target="tpu_custom_call" | custom-call | flops 3221225472 | bytes 9437184 | tf_op jit(solution)/shard_map/pallas_call | solution.py:103
  177.0 25.5 %collective-permute-done.16.refs_8_ = f32[256,1024]{1,0:T(8,128)S(1)} collective-permute-done((f32[256,1024]{1,0:T(8,128)}, f32[256,1024]{1,0:T(8,128)S(1)}, u32[]{:S(2)}, u32[]{:S(2)}) %collective-permute-start.16) | collective-permute-done | bytes 1048608 | tf_op jit(solution)/shard_map/ppermute | solution.py:24
  211.0 6.0 %shard_map.32 = f32[4,16,16,512]{3,2,1,0:T(8,128)} custom-call(bf16[256,1024]{1,0:T(8,128)(2,1)S(1)} %copy-done.23, bf16[256,1024]{1,0:T(8,128)(2,1)S(1)} %copy-done.26, bf16[256,1024]{1,0:T(8,128)(2,1)S(1)} %copy-done.5, bf16[256,1024]{1,0:T(8,128)(2,1)S(1)} %copy-done.8, bf16[256,1024]{1,0:T(8,128)(2,1)S(1)} %copy-done.11, ...), custom_call_target="tpu_custom_call" | custom-call | flops 3221225472 | bytes 9437184 | tf_op jit(solution)/shard_map/pallas_call | solution.py:103
  221.6 35.0 %all_to_all.15.part = f32[16,16,1024]{2,1,0:T(8,128)S(1)} all-to-all(f32[16,16,1024]{2,1,0:T(8,128)S(1)} %pad_maximum_fusion), channel_id=1, replica_groups=mesh['zh'=4,'y'=4,'zl'=2,'c'=2,'x'=4] {'zh','y'}, dimensions={0} | all-to-all | bytes 2097152 | tf_op jit(solution)/shard_map/all_to_all | solution.py:178
  256.5 5.8 %all-to-all-start.1 = ((f32[16,16,512]{2,1,0:T(8,128)}), f32[16,16,512]{2,1,0:T(8,128)S(1)}, u32[]{:S(2)}, u32[]{:S(2)}) async-start(f32[16,16,512]{2,1,0:T(8,128)} %bitcast.13), calls=%async_computation.3 | async-start | bytes 1048576 | tf_op jit(solution)/shard_map/all_to_all | solution.py:178
  262.3 14.1 %all-to-all-done.1.part = f32[16,16,512]{2,1,0:T(8,128)S(1)} async-done(((f32[16,16,512]{2,1,0:T(8,128)}), f32[16,16,512]{2,1,0:T(8,128)S(1)}, u32[]{:S(2)}, u32[]{:S(2)}) %all-to-all-start.1) | async-done | bytes 524320 | tf_op jit(solution)/shard_map/all_to_all | solution.py:178
  276.5 5.5 %all-to-all-start = ((f32[16,16,512]{2,1,0:T(8,128)}), f32[16,16,512]{2,1,0:T(8,128)S(1)}, u32[]{:S(2)}, u32[]{:S(2)}) async-start(f32[16,16,512]{2,1,0:T(8,128)} %bitcast.14), calls=%async_computation.1 | async-start | bytes 1048576 | tf_op jit(solution)/shard_map/all_to_all | solution.py:178
  282.0 10.9 %shard_map.34.rest_0_ = f32[4,4,32768]{2,1,0:T(4,128)} custom-call(s32[3]{0:T(128)S(1)} %pad_add_fusion.place, f32[16,16,1024]{2,1,0:T(8,128)S(1)} %all_to_all.15.part), custom_call_target="tpu_custom_call" | custom-call | bytes 2097152 | tf_op jit(solution)/shard_map/pallas_call | solution.py:125
  292.8 10.9 %shard_map.35.rest_0_ = f32[4,4,32768]{2,1,0:T(4,128)} custom-call(s32[3]{0:T(128)S(1)} %pad_add_fusion.place, f32[16,16,512]{2,1,0:T(8,128)S(1)} %all-to-all-done.1.part, f32[4,4,32768]{2,1,0:T(4,128)} %shard_map.34.rest_0_), custom_call_target="tpu_custom_call", output_to_operand_aliasing={{}: (2, {})} | custom-call | bytes 1048576 | tf_op jit(solution)/shard_map/pallas_call | solution.py:125
  303.7 10.9 %shard_map.36 = f32[4,4,32768]{2,1,0:T(4,128)} custom-call(s32[3]{0:T(128)S(1)} %pad_add_fusion.place, f32[16,16,512]{2,1,0:T(8,128)S(1)} %all-to-all-done.part, f32[4,4,32768]{2,1,0:T(4,128)} %shard_map.35.rest_0_), custom_call_target="tpu_custom_call", output_to_operand_aliasing={{}: (2, {})} | custom-call | bytes 1048576 | tf_op jit(solution)/shard_map/pallas_call | solution.py:125
  (105 shorter events, 45.3 us)
Async XLA Ops:
  6.5 210.6 %reduce-scatter.13.cloned.1.call-start = ((), (), s32[]{:S(2)}) async-start(), calls=%async_computation.12 | async-start | bytes 1310720 | tf_op jit(solution)/shard_map/reduce_scatter | solution.py:169
  6.5 37.2 %collective-permute-start.3 = (f32[512,1024]{1,0:T(8,128)}, f32[512,1024]{1,0:T(8,128)}, u32[]{:S(2)}, u32[]{:S(2)}) collective-permute-start(f32[512,1024]{1,0:T(8,128)} %w0.7), channel_id=1, source_target_pairs={{0,4},{1,5},{2,6},{3,7},{4,0},{5,1},{6,2},{7,3},{8,12},{9,13},{10,... | collective-permute-start | bytes 6291464 | tf_op jit(solution)/shard_map/ppermute | solution.py:24
  9.8 14.7 %collective-permute-start.4 = (f32[16,4,1024]{2,1,0:T(4,128)}, f32[16,4,1024]{2,1,0:T(4,128)S(1)}, u32[]{:S(2)}, u32[]{:S(2)}) collective-permute-start(f32[16,4,1024]{2,1,0:T(4,128)} %bitcast.6), channel_id=1, source_target_pairs={{0,192},{1,193},{2,194},{3,195},{4,196},{5,197},{6,198},{7,199},{8... | collective-permute-start | bytes 786440 | tf_op jit(solution)/shard_map/ppermute | solution.py:24
  24.5 9.4 %collective-permute-start.5 = (f32[16,4,1024]{2,1,0:T(4,128)S(1)}, f32[16,4,1024]{2,1,0:T(4,128)S(1)}, u32[]{:S(2)}, u32[]{:S(2)}) collective-permute-start(f32[16,4,1024]{2,1,0:T(4,128)S(1)} %collective-permute-done.4.s0), channel_id=1, source_target_pairs={{0,48},{1,49},{2,50},{3,51},{4,52},{5,53},{6,54},{7,55},{8,56},{9,... | collective-permute-start | bytes 786440 | tf_op jit(solution)/shard_map/ppermute | solution.py:24
  28.3 8.1 %collective-permute-start.6 = (f32[16,4,1024]{2,1,0:T(4,128)S(1)}, f32[16,4,1024]{2,1,0:T(4,128)S(1)}, u32[]{:S(2)}, u32[]{:S(2)}) collective-permute-start(f32[16,4,1024]{2,1,0:T(4,128)S(1)} %collective-permute-done.4.s0), channel_id=1, source_target_pairs={{0,32},{1,33},{2,34},{3,35},{4,36},{5,37},{6,38},{7,39},{8,40},{9,... | collective-permute-start | bytes 786440 | tf_op jit(solution)/shard_map/ppermute | solution.py:24
  28.7 15.0 %collective-permute-start.7 = (f32[16,4,1024]{2,1,0:T(4,128)S(1)}, f32[16,4,1024]{2,1,0:T(4,128)S(1)}, u32[]{:S(2)}, u32[]{:S(2)}) collective-permute-start(f32[16,4,1024]{2,1,0:T(4,128)S(1)} %collective-permute-done.4.s0), channel_id=1, source_target_pairs={{0,16},{1,17},{2,18},{3,19},{4,20},{5,21},{6,22},{7,23},{8,24},{9,... | collective-permute-start | bytes 786440 | tf_op jit(solution)/shard_map/ppermute | solution.py:24
  45.3 34.4 %copy-start.1 = (f32[512,1024]{1,0:T(8,128)S(1)}, f32[512,1024]{1,0:T(8,128)}, u32[]{:S(2)}) copy-start(f32[512,1024]{1,0:T(8,128)} %w0.7) | copy-start | bytes 6291460
  52.9 165.3 %reduce-scatter.15.cloned.1.call-start = ((), (), s32[]{:S(2)}) async-start(), calls=%async_computation.13 | async-start | bytes 1310720 | tf_op jit(solution)/shard_map/reduce_scatter | solution.py:169
  52.9 11.4 %collective-permute-start.8 = (f32[16,4,1024]{2,1,0:T(4,128)S(1)}, f32[16,4,1024]{2,1,0:T(4,128)S(1)}, u32[]{:S(2)}, u32[]{:S(2)}) collective-permute-start(f32[16,4,1024]{2,1,0:T(4,128)S(1)} %bitcast.7), channel_id=1, source_target_pairs={{0,128},{1,129},{2,130},{3,131},{4,132},{5,133},{6,134},{7,135},{8... | collective-permute-start | bytes 786440 | tf_op jit(solution)/shard_map/ppermute | solution.py:24
  64.4 8.0 %collective-permute-start.10 = (f32[16,4,1024]{2,1,0:T(4,128)S(1)}, f32[16,4,1024]{2,1,0:T(4,128)S(1)}, u32[]{:S(2)}, u32[]{:S(2)}) collective-permute-start(f32[16,4,1024]{2,1,0:T(4,128)S(1)} %collective-permute-done.8.s0), channel_id=1, source_target_pairs={{0,32},{1,33},{2,34},{3,35},{4,36},{5,37},{6,38},{7,39},{8,40},{9,... | collective-permute-start | bytes 786440 | tf_op jit(solution)/shard_map/ppermute | solution.py:24
  64.7 15.0 %collective-permute-start.11 = (f32[16,4,1024]{2,1,0:T(4,128)S(1)}, f32[16,4,1024]{2,1,0:T(4,128)S(1)}, u32[]{:S(2)}, u32[]{:S(2)}) collective-permute-start(f32[16,4,1024]{2,1,0:T(4,128)S(1)} %collective-permute-done.8.s0), channel_id=1, source_target_pairs={{0,16},{1,17},{2,18},{3,19},{4,20},{5,21},{6,22},{7,23},{8,24},{9,... | collective-permute-start | bytes 786440 | tf_op jit(solution)/shard_map/ppermute | solution.py:24
  64.7 15.0 %collective-permute-start.9 = (f32[16,4,1024]{2,1,0:T(4,128)S(1)}, f32[16,4,1024]{2,1,0:T(4,128)S(1)}, u32[]{:S(2)}, u32[]{:S(2)}) collective-permute-start(f32[16,4,1024]{2,1,0:T(4,128)S(1)} %collective-permute-done.8.s0), channel_id=1, source_target_pairs={{0,48},{1,49},{2,50},{3,51},{4,52},{5,53},{6,54},{7,55},{8,56},{9,... | collective-permute-start | bytes 786440 | tf_op jit(solution)/shard_map/ppermute | solution.py:24
  86.3 132.9 %reduce-scatter.17.cloned.1.call-start = ((), (), s32[]{:S(2)}) async-start(), calls=%async_computation.14 | async-start | bytes 1310720 | tf_op jit(solution)/shard_map/reduce_scatter | solution.py:169
  86.3 20.8 %collective-permute-start.12 = (f32[16,4,1024]{2,1,0:T(4,128)S(1)}, f32[16,4,1024]{2,1,0:T(4,128)S(1)}, u32[]{:S(2)}, u32[]{:S(2)}) collective-permute-start(f32[16,4,1024]{2,1,0:T(4,128)S(1)} %bitcast.8), channel_id=1, source_target_pairs={{0,64},{1,65},{2,66},{3,67},{4,68},{5,69},{6,70},{7,71},{8,72},{9,... | collective-permute-start | bytes 786440 | tf_op jit(solution)/shard_map/ppermute | solution.py:24
  107.1 7.5 %collective-permute-start.13 = (f32[16,4,1024]{2,1,0:T(4,128)S(1)}, f32[16,4,1024]{2,1,0:T(4,128)S(1)}, u32[]{:S(2)}, u32[]{:S(2)}) collective-permute-start(f32[16,4,1024]{2,1,0:T(4,128)S(1)} %collective-permute-done.12.s0), channel_id=1, source_target_pairs={{0,48},{1,49},{2,50},{3,51},{4,52},{5,53},{6,54},{7,55},{8,56},{9,... | collective-permute-start | bytes 786440 | tf_op jit(solution)/shard_map/ppermute | solution.py:24
  107.1 9.0 %collective-permute-start.14 = (f32[16,4,1024]{2,1,0:T(4,128)S(1)}, f32[16,4,1024]{2,1,0:T(4,128)S(1)}, u32[]{:S(2)}, u32[]{:S(2)}) collective-permute-start(f32[16,4,1024]{2,1,0:T(4,128)S(1)} %collective-permute-done.12.s0), channel_id=1, source_target_pairs={{0,32},{1,33},{2,34},{3,35},{4,36},{5,37},{6,38},{7,39},{8,40},{9,... | collective-permute-start | bytes 786440 | tf_op jit(solution)/shard_map/ppermute | solution.py:24
  107.5 15.0 %collective-permute-start.15 = (f32[16,4,1024]{2,1,0:T(4,128)S(1)}, f32[16,4,1024]{2,1,0:T(4,128)S(1)}, u32[]{:S(2)}, u32[]{:S(2)}) collective-permute-start(f32[16,4,1024]{2,1,0:T(4,128)S(1)} %collective-permute-done.12.s0), channel_id=1, source_target_pairs={{0,16},{1,17},{2,18},{3,19},{4,20},{5,21},{6,22},{7,23},{8,24},{9,... | collective-permute-start | bytes 786440 | tf_op jit(solution)/shard_map/ppermute | solution.py:24
  129.8 90.4 %reduce-scatter.11.cloned.1.call-start = ((), (), s32[]{:S(2)}) async-start(), calls=%async_computation.11 | async-start | bytes 1310720 | tf_op jit(solution)/shard_map/reduce_scatter | solution.py:169
  129.9 7.5 %collective-permute-start = (f32[16,4,1024]{2,1,0:T(4,128)S(1)}, f32[16,4,1024]{2,1,0:T(4,128)S(1)}, u32[]{:S(2)}, u32[]{:S(2)}) collective-permute-start(f32[16,4,1024]{2,1,0:T(4,128)S(1)} %bitcast.9), channel_id=1, source_target_pairs={{0,48},{1,49},{2,50},{3,51},{4,52},{5,53},{6,54},{7,55},{8,56},{9,... | collective-permute-start | bytes 786440 | tf_op jit(solution)/shard_map/ppermute | solution.py:24
  130.0 7.8 %collective-permute-start.1 = (f32[16,4,1024]{2,1,0:T(4,128)S(1)}, f32[16,4,1024]{2,1,0:T(4,128)S(1)}, u32[]{:S(2)}, u32[]{:S(2)}) collective-permute-start(f32[16,4,1024]{2,1,0:T(4,128)S(1)} %bitcast.10), channel_id=1, source_target_pairs={{0,32},{1,33},{2,34},{3,35},{4,36},{5,37},{6,38},{7,39},{8,40},{9,... | collective-permute-start | bytes 786440 | tf_op jit(solution)/shard_map/ppermute | solution.py:24
  130.4 15.0 %collective-permute-start.2 = (f32[16,4,1024]{2,1,0:T(4,128)S(1)}, f32[16,4,1024]{2,1,0:T(4,128)S(1)}, u32[]{:S(2)}, u32[]{:S(2)}) collective-permute-start(f32[16,4,1024]{2,1,0:T(4,128)S(1)} %bitcast.11), channel_id=1, source_target_pairs={{0,16},{1,17},{2,18},{3,19},{4,20},{5,21},{6,22},{7,23},{8,24},{9,... | collective-permute-start | bytes 786440 | tf_op jit(solution)/shard_map/ppermute | solution.py:24
  132.9 23.7 %collective-permute-start.18 = (f32[256,1024]{1,0:T(8,128)}, f32[256,1024]{1,0:T(8,128)S(1)}, u32[]{:S(2)}, u32[]{:S(2)}) collective-permute-start(f32[256,1024]{1,0:T(8,128)} %get-tuple-element.29), channel_id=1, source_target_pairs={{0,200},{1,201},{2,202},{3,203},{4,204},{5,205},{6,206},{7,207},{8... | collective-permute-start | bytes 3145736 | tf_op jit(solution)/shard_map/ppermute | solution.py:24
  152.8 103.7 %reduce-scatter.9.cloned.1.call-start = ((), (), s32[]{:S(2)}) async-start(), calls=%async_computation.10 | async-start | bytes 2621440 | tf_op jit(solution)/shard_map/reduce_scatter | solution.py:169
  156.6 4.4 %collective-permute-start.19 = (f32[256,1024]{1,0:T(8,128)S(1)}, f32[256,1024]{1,0:T(8,128)S(1)}, u32[]{:S(2)}, u32[]{:S(2)}) collective-permute-start(f32[256,1024]{1,0:T(8,128)S(1)} %collective-permute-done.18.refs_8_), channel_id=1, source_target_pairs={{0,4},{1,5},{2,6},{3,7},{4,0},{5,1},{6,2},{7,3},{8,12},{9,13},{10,... | collective-permute-start | bytes 3145736 | tf_op jit(solution)/shard_map/ppermute | solution.py:24
  176.4 30.4 %copy-start.8 = (bf16[256,1024]{1,0:T(8,128)(2,1)S(1)}, bf16[256,1024]{1,0:T(8,128)(2,1)}, u32[]{:S(2)}) copy-start(bf16[256,1024]{1,0:T(8,128)(2,1)} %copy-done.6) | copy-start | bytes 1572868
  176.4 30.4 %copy-start.11 = (bf16[256,1024]{1,0:T(8,128)(2,1)S(1)}, bf16[256,1024]{1,0:T(8,128)(2,1)}, u32[]{:S(2)}) copy-start(bf16[256,1024]{1,0:T(8,128)(2,1)} %copy-done.9) | copy-start | bytes 1572868
  176.4 30.4 %copy-start.14 = (bf16[256,1024]{1,0:T(8,128)(2,1)S(1)}, bf16[256,1024]{1,0:T(8,128)(2,1)}, u32[]{:S(2)}) copy-start(bf16[256,1024]{1,0:T(8,128)(2,1)} %copy-done.12) | copy-start | bytes 1572868
  176.4 85.9 %reduce-scatter.7.cloned.1.call-start = ((), (), s32[]{:S(2)}) async-start(), calls=%async_computation.9 | async-start | bytes 2621440 | tf_op jit(solution)/shard_map/reduce_scatter | solution.py:169
  176.5 26.0 %collective-permute-start.16 = (f32[256,1024]{1,0:T(8,128)}, f32[256,1024]{1,0:T(8,128)S(1)}, u32[]{:S(2)}, u32[]{:S(2)}) collective-permute-start(f32[256,1024]{1,0:T(8,128)} %get-tuple-element.30), channel_id=1, source_target_pairs={{0,8},{1,9},{2,10},{3,11},{4,12},{5,13},{6,14},{7,15},{8,64},{9,65... | collective-permute-start | bytes 3145736 | tf_op jit(solution)/shard_map/ppermute | solution.py:24
  202.5 3.4 %collective-permute-start.17 = (f32[256,1024]{1,0:T(8,128)S(1)}, f32[256,1024]{1,0:T(8,128)S(1)}, u32[]{:S(2)}, u32[]{:S(2)}) collective-permute-start(f32[256,1024]{1,0:T(8,128)S(1)} %collective-permute-done.16.refs_8_), channel_id=1, source_target_pairs={{0,4},{1,5},{2,6},{3,7},{4,0},{5,1},{6,2},{7,3},{8,12},{9,13},{10,... | collective-permute-start | bytes 3145736 | tf_op jit(solution)/shard_map/ppermute | solution.py:24
  256.5 19.9 %all-to-all-start.1 = ((f32[16,16,512]{2,1,0:T(8,128)}), f32[16,16,512]{2,1,0:T(8,128)S(1)}, u32[]{:S(2)}, u32[]{:S(2)}) async-start(f32[16,16,512]{2,1,0:T(8,128)} %bitcast.13), calls=%async_computation.3 | async-start | bytes 1048576 | tf_op jit(solution)/shard_map/all_to_all | solution.py:178
  276.5 27.2 %all-to-all-start = ((f32[16,16,512]{2,1,0:T(8,128)}), f32[16,16,512]{2,1,0:T(8,128)S(1)}, u32[]{:S(2)}, u32[]{:S(2)}) async-start(f32[16,16,512]{2,1,0:T(8,128)} %bitcast.14), calls=%async_computation.1 | async-start | bytes 1048576 | tf_op jit(solution)/shard_map/all_to_all | solution.py:178
  (25 other events, 80.7 us)
Sparse Core Ops, SparseCore 0:
  53.0 22.3 reduce-scatter.12
  86.4 27.7 reduce-scatter.14
  130.0 21.3 reduce-scatter.16
  153.9 25.8 reduce-scatter.10
  182.2 33.3 reduce-scatter.8
  218.2 31.9 reduce-scatter.6

commit v2 on v0

v2 whole, which is shorter than its diff:
```python
import functools

import jax
import jax.numpy as jnp
import numpy as np
from jax import lax
from jax.experimental import pallas as pl
from jax.experimental.pallas import tpu as pltpu
from jax.sharding import Mesh
from jax.sharding import PartitionSpec as P

AXES = ("zh", "y", "zl", "c", "x")
SIZES = (4, 4, 2, 2, 4)
VMEM = pl.BlockSpec(memory_space=pltpu.VMEM)
SMEM = pl.BlockSpec(memory_space=pltpu.SMEM)
HBM = pl.BlockSpec(memory_space=pltpu.MemorySpace.HBM)
F32, BF16 = jnp.float32, jnp.bfloat16


def move(value, x=0, y=0, z=0, c=0, apart=0):
    pairs = []
    for source, (at_zh, at_y, at_zl, at_c, at_x) in enumerate(np.ndindex(*SIZES)):
        to_z = (2 * at_zh + at_zl + z + (2 * at_c - 1) * apart) % 8
        to = (to_z // 2, (at_y + y) % 4, to_z % 2, (at_c + c) % 2, (at_x + x) % 4)
        pairs.append((source, int(np.ravel_multi_index(to, SIZES))))
    return lax.ppermute(value, AXES, pairs)


def after(value, *others):
    return lax.optimization_barrier((value, others))[0]


def call(kernel, args, shapes, scratch=(), place=None, in_hbm=(), out_hbm=(), aliases=None, limit=12):
    count = len(args)
    specs = [HBM if n in in_hbm else VMEM for n in range(count)]
    if place is not None:
        args, specs = [place, *args], [SMEM, *specs]
    return pl.pallas_call(
        kernel,
        in_specs=specs,
        out_specs=[HBM if n in out_hbm else VMEM for n in range(len(shapes))],
        out_shape=[jax.ShapeDtypeStruct(*shape) for shape in shapes],
        scratch_shapes=list(scratch),
        input_output_aliases=aliases or {},
        compiler_params=pltpu.CompilerParams(vmem_limit_bytes=limit * 2**20),
        cost_estimate=pl.CostEstimate(flops=0, bytes_accessed=0, transcendentals=0),
    )(*args)


def split(value):
    high = value.astype(BF16)
    return high, (value - high.astype(F32)).astype(BF16)


def turn_kernel(place, value, out):
    for j in range(4):
        out[j] = value[:, j, :]


def halved_kernel(value, high, low):
    high[...], low[...] = split(value[...])


def halved(value):
    return call(halved_kernel, [value], [(value.shape, BF16)] * 2)


def pair_kernel(one, other, out):
    out[0] = one[...]
    out[1] = other[...]


def pair(one, other):
    return call(pair_kernel, [one, other], [((2, *one.shape), F32)])[0]


def forward_kernel(own, low, high, to_right, to_left):
    for out, come, start in ((to_right, low, 0), (to_left, high, 8)):
        out[:, :16] = own[...]
        out[:, 16:24] = come[0, :, start : start + 8]
        out[:, 24:] = come[1, :, start : start + 8]


def forward(own, low, high):
    shape = (4, 32, own.shape[2])
    to_right, to_left = call(forward_kernel, [own, low, high], [(shape, F32)] * 2)
    return move(to_right, y=1), move(to_left, y=-1)


def product(t_high, t_low, w_high, w_low):
    dot = functools.partial(lax.dot_general, dimension_numbers=(((1,), (1,)), ((), ())), preferred_element_type=F32)
    return dot(t_high, w_high) + (dot(t_high, w_low) + dot(t_low, w_high))


def store(blocks, at, outs):
    half = blocks.shape[1] // 2
    columns = slice(at, at + blocks.shape[2])
    to_right, to_left, right_low, left_high, own = outs
    to_right[:half, columns] = blocks[2, :half]
    to_right[half:, columns] = blocks[1, half:]
    to_left[:half, columns] = blocks[2, half:]
    to_left[half:, columns] = blocks[3, :half]
    right_low[:, columns] = blocks[1, :half]
    left_high[:, columns] = blocks[3, half:]
    own[:, columns] = blocks[0]


def shapes_of(rows, columns):
    return [((n, columns), F32) for n in (rows, rows, rows // 2, rows // 2, rows)]


def first_kernel(sources, n_parts, place, *refs):
    n = len(sources)
    parts, ws, outs = refs[:n_parts], refs[n_parts : n_parts + 4], refs[n_parts + 4 : n_parts + 9]
    split_t, t = refs[n_parts + 9 : -1], refs[-1]
    for g, group in enumerate(sources):
        for d, halves in enumerate(group):
            at = lax.rem(place[0] + d, 4)
            for x in range(4):
                number, lead, start = halves[x // 2]
                part = parts[number] if lead is None else parts[number].at[lead]
                start = start + 4 * (x % 2)
                e = lax.rem(x - place[3] + 4, 4)
                for j in range(4):
                    t[e, at, 4 * j : 4 * j + 4, :] = part[j, start : start + 4, :]
        split_t[2 * g][...], split_t[2 * g + 1][...] = split(t[...].reshape(256, -1))
    for k in range(4):
        rows = slice(256 * (k % 2), 256 * (k % 2) + 256)
        w_high, w_low = ws[k // 2 * 2][rows, :], ws[k // 2 * 2 + 1][rows, :]
        blocks = [product(split_t[2 * g][...], split_t[2 * g + 1][...], w_high, w_low) for g in range(n)]
        blocks = [block.reshape(4, 64, 256) for block in blocks]
        store(blocks[0] if n == 1 else jnp.concatenate(blocks, axis=1), 256 * k, outs)


def first(place, sources, parts, w0, w1):
    kc, n = w0[0].shape[1], len(sources)
    out = call(
        functools.partial(first_kernel, sources, len(parts)),
        [*parts, *w0, *w1],
        shapes_of(64 * n, 1024) + [((256, kc), BF16)] * (2 * n),
        [pltpu.VMEM((4, 4, 16, kc), F32)],
        place,
        limit=16,
    )
    return out[:5], [out[5 + 2 * g : 7 + 2 * g] for g in range(n)]


def second_kernel(half, place, *refs):
    groups, w, (out, buffer, sems) = refs[:8], refs[8], refs[-3:]
    copies = []
    for n in range(2):
        w_high, w_low = split(w[256 * n : 256 * n + 256, :])
        for d in range(4):
            block = product(groups[2 * d][...], groups[2 * d + 1][...], w_high, w_low)
            buffer[n, :, :, 4 * d : 4 * d + 4, :] = block.reshape(4, 16, 4, 256)
        for e in range(4):
            to = out.at[lax.rem(place[3] + e, 4), :, :, pl.ds(512 * half + 256 * n, 256)]
            copies.append(pltpu.make_async_copy(buffer.at[n, e], to, sems.at[n, e]))
            copies[-1].start()
    for copy in copies:
        copy.wait()


def second(place, groups, w, half, out=None):
    args = [g for pair in groups for g in pair] + [w]
    return call(
        functools.partial(second_kernel, half),
        args if out is None else [*args, out],
        [((4, 16, 16, 1024), F32)],
        [pltpu.VMEM((2, 4, 16, 16, 256), F32), pltpu.SemaphoreType.DMA((2, 4))],
        place,
        in_hbm=(9,),
        out_hbm=(0,),
        aliases=None if out is None else {10: 0},
    )[0]


def add_kernel(right_low, left_high, from_left, from_right, to_right, to_left):
    half = right_low.shape[0]
    to_right[...] = right_low[...] + from_left[:half]
    to_left[...] = left_high[...] + from_right[:half]


def ring_first(parts):
    return move(parts[0], x=1), move(parts[1], x=-1)


def ring_second(parts, come):
    to_right, to_left = call(add_kernel, [*parts[2:4], *come], [(parts[2].shape, F32)] * 2)
    return [parts[4], *come, move(to_right, x=1), move(to_left, x=-1)]


def total(own, from_left, from_right, from_left2, from_right2):
    half = own.shape[0] // 2
    low = own[:half] + from_right[half:] + from_left2[...]
    high = own[half:] + from_left[half:] + from_right2[...]
    return jnp.concatenate([low, high])


def collect_kernel(*refs):
    out = refs[-1]
    sums = [total(*refs[5 * u : 5 * u + 5]) for u in range(3)]
    for d, value in enumerate([sums[0], sums[1][:64], sums[2], sums[1][64:]]):
        out[:, 4 * d : 4 * d + 4, :] = value.reshape(16, 4, -1)


def collect(sums):
    return call(collect_kernel, [term for terms in sums for term in terms], [((16, 16, 1024), F32)])[0]


def place_kernel(column, n_parts, place, *refs):
    parts, (out, block, done) = refs[:n_parts], refs[-3:]
    pieces = [(part, at) for part in parts for at in range(0, part.shape[2], 512)]
    copies = []
    for s in range(16):
        for q, (part, at) in enumerate(pieces):
            for d in range(4):
                block[q, s, :, (s // 4 + d) % 4, :] = part[s, 4 * d : 4 * d + 4, at : at + 512]
            columns = pl.ds(pl.multiple_of(512 * column(place, s, q), 512), 512)
            copies.append(pltpu.make_async_copy(block.at[q, s], out.at[:, :, columns], done.at[16 * q + s]))
            copies[-1].start()
    for copy in copies:
        copy.wait()


def placed(place, parts, column, out=None):
    n = sum(part.shape[2] // 512 for part in parts)
    return call(
        functools.partial(place_kernel, column, len(parts)),
        parts if out is None else [*parts, out],
        [((4, 4, 32768), F32)],
        [pltpu.VMEM((n, 16, 4, 4, 512), F32), pltpu.SemaphoreType.DMA((16 * n,))],
        place,
        in_hbm=(len(parts),),
        out_hbm=(0,),
        aliases=None if out is None else {1 + len(parts): 0},
    )[0]


def own_column(place, s, q):
    return s * 4 + place[1] * 2 + lax.rem(place[2] + q, 2)


def next_column(place, s, q):
    core = lax.rem(place[2] + q, 2)
    z = lax.rem(2 * (s // 4) + place[1] + 9 - 2 * core, 8)
    return ((z // 2) * 4 + s % 4) * 4 + lax.rem(z, 2) * 2 + core


def shards(integrals, amplitudes):
    place = jnp.stack([lax.axis_index(n).astype(jnp.int32) for n in ("y", "zl", "c", "x")])
    kc = integrals.shape[1]
    (t0,) = call(turn_kernel, [jnp.transpose(amplitudes, (1, 2, 0))], [((4, 16, kc), F32)], place=place)

    t1, t3 = move(t0, z=-2), move(t0, z=2)
    low0, high0, far0 = move(t0, y=1), move(t0, y=-1), move(t0, y=2)
    w = halved(integrals)

    t1, t3, low0, high0, far0 = after((t1, t3, low0, high0, far0))
    w1 = move(after(integrals, t1), c=1)
    t13 = pair(t1, t3)
    low13, high13 = move(t13, y=1), move(t13, y=-1)
    t2 = move(after(t0, t1), z=4)
    w1 = halved(w1)

    def whole(n, lead=None):
        return ((n, lead, 0), (n, lead, 8))

    def halves(at):
        return ((2, None, at), (3, None, at))

    parts0, (group0,) = first(place, [[whole(n) for n in range(4)]], [t0, high0, far0, low0], w, w1)
    come0 = ring_first(parts0)

    t2, low13, high13 = after((t2, low13, high13), parts0, come0)
    w2 = move(after(integrals, t2), apart=1)
    low2, high2 = forward(t2, low13, high13)
    far2 = move(t2, y=2)
    sum0 = ring_second(parts0, come0)
    low2, high2, far2 = after((low2, high2, far2))
    sources = [[whole(0, g), whole(1, g), halves(16 + 8 * g), whole(4, g)] for g in range(2)]
    parts1, (group1, group3) = first(place, sources, [t13, high13, low2, high2, low13], w, w1)
    come1 = ring_first(parts1)
    parts2, (group2,) = first(place, [[whole(n) for n in range(4)]], [after(t2, parts1), high2, far2, low2], w, w1)
    come2 = ring_first(parts2)
    w3 = move(after(w2, parts1), c=1)

    groups = [group0, group1, group2, group3]
    both = second(place, groups, after(w2, sum0), 0)
    both = second(place, groups, after(w3, both, come1), 1, both)
    rest = lax.psum_scatter(both, "x", scatter_dimension=0)
    sum1 = ring_second(after(parts1, both), come1)
    sum2 = ring_second(after(parts2, both), come2)

    def relaid(value):
        return lax.all_to_all(value, ("zh", "y"), split_axis=0, concat_axis=0, tiled=True)

    out = placed(place, [relaid(collect([sum0, sum1, sum2]))], own_column)
    return placed(place, [relaid(rest)], next_column, out)


def solution(mesh):
    fine = Mesh(mesh.devices.reshape(SIZES), AXES)
    return jax.shard_map(
        shards,
        mesh=fine,
        in_specs=(P(("zh", "y", "zl", "c"), "x"), P("x", ("zl", "c"), ("zh", "y"))),
        out_specs=P(("zl", "c", "x"), ("zh", "y"), None),
        check_vma=False,
    )
```

time: 360 us -> 209 us (0.58)
  the two profiles are of different devices: /device:TPU:1 before, /device:TPU:38 now
where the time goes in v2:
time: 209 us
  waiting for transfers between devices  92.4 us (44%)
  starting transfers between devices  41.9 us (20%)
  blocking collectives  31.5 us (15%)
  Pallas kernels  23.8 us (11%)
  between operations  13.6 us (7%)
  local copies, waits for them, and re-layouts  5.46 us (3%)
    ppermute x26, waiting for transfers between devices, move(): return lax.ppermute(value, AXES, pairs)  64.7 us
    ppermute x26, starting transfers between devices, move(): return lax.ppermute(value, AXES, pairs)  37.7 us
    all_to_all x1, blocking collectives, relaid(): lax.all_to_all(value, ('zh', 'y'), split_axis=0, concat_axis=0, tiled=True)  31.5 us
    all_to_all x1, waiting for transfers between devices, relaid(): lax.all_to_all(value, ('zh', 'y'), split_axis=0, concat_axis=0, tiled=True)  27.7 us
    pallas_call x16, Pallas kernels, call(): pl.pallas_call(kernel, in_specs=specs, out_specs=[HBM if n in out_hbm els...  23.8 us
    unnamed x16, local copies, waits for them, and re-layouts  5.46 us
    all_to_all x1, starting transfers between devices, relaid(): lax.all_to_all(value, ('zh', 'y'), split_axis=0, concat_axis=0, tiled=True)  4.22 us
  transfers between devices with their start and end apart: 28, of which 14 were waited for; matrix products, arithmetic and copies ran while one was open for 0% of the time, Pallas kernels for 8%

profile of v2, /device:TPU:38, one launch (start us, length us, event | category | flops | bytes accessed | tf_op | source)
XLA Modules:
  0.0 208.8 jit_solution(180555374880842488)
XLA Ops:
  8.2 5.5 %collective-permute-start = (f32[4,16,1024]{2,1,0:T(8,128)S(1)}, f32[4,16,1024]{2,1,0:T(8,128)S(1)}, u32[]{:S(2)}, u32[]{:S(2)}) collective-permute-start(f32[4,16,1024]{2,1,0:T(8,128)S(1)} %shard_map.28.refs_0_), channel_id=1, source_target_pairs={{0,192},{1,193},{2,194},{3,195},{4,196},{5,197},{6,198},{7,199},{8... | collective-permute-start | bytes 786440 | tf_op jit(solution)/shard_map/ppermute | solution.py:26
  15.2 1.7 collective-permute-start.3
  16.9 2.0 collective-permute-start.4
  18.9 4.5 %collective-permute-done.one = f32[4,16,1024]{2,1,0:T(8,128)S(1)} collective-permute-done((f32[4,16,1024]{2,1,0:T(8,128)S(1)}, f32[4,16,1024]{2,1,0:T(8,128)S(1)}, u32[]{:S(2)}, u32[]{:S(2)}) %collective-permute-start) | collective-permute-done | bytes 262176 | tf_op jit(solution)/shard_map/ppermute | solution.py:26
  23.4 5.7 %collective-permute-done.1.other = f32[4,16,1024]{2,1,0:T(8,128)S(1)} collective-permute-done((f32[4,16,1024]{2,1,0:T(8,128)S(1)}, f32[4,16,1024]{2,1,0:T(8,128)S(1)}, u32[]{:S(2)}, u32[]{:S(2)}) %collective-permute-start.1) | collective-permute-done | bytes 262176 | tf_op jit(solution)/shard_map/ppermute | solution.py:26
  30.9 1.9 collective-permute-start.8
  32.8 1.6 copy-done.1
  34.8 3.6 %collective-permute-start.6 = (f32[4,16,1024]{2,1,0:T(8,128)S(1)}, f32[4,16,1024]{2,1,0:T(8,128)S(1)}, u32[]{:S(2)}, u32[]{:S(2)}) collective-permute-start(f32[4,16,1024]{2,1,0:T(8,128)S(1)} %shard_map.28.refs_0_), channel_id=1, source_target_pairs={{0,128},{1,129},{2,130},{3,131},{4,132},{5,133},{6,134},{7,135},{8... | collective-permute-start | bytes 786440 | tf_op jit(solution)/shard_map/ppermute | solution.py:26
  38.7 2.6 %shard_map.31 = (f32[64,1024]{1,0:T(8,128)S(1)}, f32[64,1024]{1,0:T(8,128)S(1)}, f32[32,1024]{1,0:T(8,128)S(1)}, f32[32,1024]{1,0:T(8,128)S(1)}, f32[64,1024]{1,...) custom-call(s32[4]{0:T(128)S(1)} %pad_add_fusion.place, ...), custom_call_target="tpu_custom_call" | custom-call | tf_op jit(solution)/shard_map/pallas_call | solution.py:38
  42.2 2.4 %collective-permute-start.9 = (f32[64,1024]{1,0:T(8,128)S(1)}, f32[64,1024]{1,0:T(8,128)S(1)}, u32[]{:S(2)}, u32[]{:S(2)}) collective-permute-start(f32[64,1024]{1,0:T(8,128)S(1)} %get-tuple-element.77), channel_id=1, source_target_pairs={{0,1},{1,2},{2,3},{3,0},{4,5},{5,6},{6,7},{7,4},{8,9},{9,10},{10,1... | collective-permute-start | bytes 786440 | tf_op jit(solution)/shard_map/ppermute | solution.py:26
  44.6 6.5 %collective-permute-done.6.own.refs_0_ = f32[4,16,1024]{2,1,0:T(8,128)S(1)} collective-permute-done((f32[4,16,1024]{2,1,0:T(8,128)S(1)}, f32[4,16,1024]{2,1,0:T(8,128)S(1)}, u32[]{:S(2)}, u32[]{:S(2)}) %collective-permute-start.6) | collective-permute-done | bytes 262176 | tf_op jit(solution)/shard_map/ppermute | solution.py:26
  51.6 3.2 %collective-permute-start.12 = (f32[4,32,1024]{2,1,0:T(8,128)S(1)}, f32[4,32,1024]{2,1,0:T(8,128)S(1)}, u32[]{:S(2)}, u32[]{:S(2)}) collective-permute-start(f32[4,32,1024]{2,1,0:T(8,128)S(1)} %get-tuple-element.86), channel_id=1, source_target_pairs={{0,48},{1,49},{2,50},{3,51},{4,52},{5,53},{6,54},{7,55},{8,56},{9,... | collective-permute-start | bytes 1572872 | tf_op jit(solution)/shard_map/ppermute | solution.py:26
  56.4 16.3 %collective-permute-done.13.refs_2_ = f32[4,16,1024]{2,1,0:T(8,128)S(1)} collective-permute-done((f32[4,16,1024]{2,1,0:T(8,128)S(1)}, f32[4,16,1024]{2,1,0:T(8,128)S(1)}, u32[]{:S(2)}, u32[]{:S(2)}) %collective-permute-start.13) | collective-permute-done | bytes 262176 | tf_op jit(solution)/shard_map/ppermute | solution.py:26
  73.1 4.5 %shard_map.34 = (f32[128,1024]{1,0:T(8,128)S(1)}, f32[128,1024]{1,0:T(8,128)S(1)}, f32[64,1024]{1,0:T(8,128)S(1)}, f32[64,1024]{1,0:T(8,128)S(1)}, f32[128,1024]...) custom-call(s32[4]{0:T(128)S(1)} %pad_add_fusion.place, ...), custom_call_target="tpu_custom_call" | custom-call | tf_op jit(solution)/shard_map/pallas_call | solution.py:38
  77.8 1.9 collective-permute-start.18
  79.8 3.2 %collective-permute-start.16 = (f32[32,1024]{1,0:T(8,128)S(1)}, f32[32,1024]{1,0:T(8,128)S(1)}, u32[]{:S(2)}, u32[]{:S(2)}) collective-permute-start(f32[32,1024]{1,0:T(8,128)S(1)} %get-tuple-element.104), channel_id=1, source_target_pairs={{0,1},{1,2},{2,3},{3,0},{4,5},{5,6},{6,7},{7,4},{8,9},{9,10},{10,1... | collective-permute-start | bytes 393224 | tf_op jit(solution)/shard_map/ppermute | solution.py:26
  83.0 2.6 %shard_map.35 = (f32[64,1024]{1,0:T(8,128)S(1)}, f32[64,1024]{1,0:T(8,128)S(1)}, f32[32,1024]{1,0:T(8,128)S(1)}, f32[32,1024]{1,0:T(8,128)S(1)}, f32[64,1024]{1,...) custom-call(s32[4]{0:T(128)S(1)} %pad_add_fusion.place, ...), custom_call_target="tpu_custom_call" | custom-call | tf_op jit(solution)/shard_map/pallas_call | solution.py:38
  85.6 9.3 %collective-permute-done.16.refs_3_ = f32[32,1024]{1,0:T(8,128)S(1)} collective-permute-done((f32[32,1024]{1,0:T(8,128)S(1)}, f32[32,1024]{1,0:T(8,128)S(1)}, u32[]{:S(2)}, u32[]{:S(2)}) %collective-permute-start.16) | collective-permute-done | bytes 131104 | tf_op jit(solution)/shard_map/ppermute | solution.py:26
  94.9 2.8 %collective-permute-done.17.refs_4_ = f32[32,1024]{1,0:T(8,128)S(1)} collective-permute-done((f32[32,1024]{1,0:T(8,128)S(1)}, f32[32,1024]{1,0:T(8,128)S(1)}, u32[]{:S(2)}, u32[]{:S(2)}) %collective-permute-start.17) | collective-permute-done | bytes 131104 | tf_op jit(solution)/shard_map/ppermute | solution.py:26
  97.7 4.5 %shard_map.37.refs_9_ = f32[4,16,16,1024]{3,2,1,0:T(8,128)S(1)} custom-call(s32[4]{0:T(128)S(1)} %pad_add_fusion.place, bf16[256,1024]{1,0:T(8,128)(2,1)S(1)} %get-tuple-element.73.refs_0_, bf16[256,1024]{1,0:T(8,128)(2,1)S(1)} %get-tuple-element.74.refs_1_, bf16[256,1024]{1,0:T(8,128)(2,1)S(1)} %get-tuple-element.89.refs_2_, ...), custom_call_target="tpu_custom_call" | custom-call | tf_op jit(solution)/shard_map/pallas_call | solution.py:38
  102.3 4.5 %shard_map.38 = f32[4,16,16,1024]{3,2,1,0:T(8,128)S(1)} custom-call(s32[4]{0:T(128)S(1)} %pad_add_fusion.place, bf16[256,1024]{1,0:T(8,128)(2,1)S(1)} %get-tuple-element.73.refs_0_, bf16[256,1024]{1,0:T(8,128)(2,1)S(1)} %get-tuple-element.74.refs_1_, bf16[256,1024]{1,0:T(8,128)(2,1)S(1)} %get-tuple-element.89.refs_2_, ...), custom_call_target="tpu_custom_call", output_to_operand_aliasing={{}: (10, {})} | custom-call | tf_op jit(solution)/shard_map/pallas_call | solution.py:38
  106.8 2.0 copy-done
  109.2 1.7 collective-permute-start.23
  113.1 5.3 %collective-permute-done.22.from_left.refs_11_ = f32[64,1024]{1,0:T(8,128)S(1)} collective-permute-done((f32[64,1024]{1,0:T(8,128)}, f32[64,1024]{1,0:T(8,128)S(1)}, u32[]{:S(2)}, u32[]{:S(2)}) %collective-permute-start.22) | collective-permute-done | bytes 262176 | tf_op jit(solution)/shard_map/ppermute | solution.py:26
  120.9 2.0 collective-permute-start.25
  122.9 8.5 %collective-permute-done.24.refs_13_ = f32[32,1024]{1,0:T(8,128)S(1)} collective-permute-done((f32[32,1024]{1,0:T(8,128)S(1)}, f32[32,1024]{1,0:T(8,128)S(1)}, u32[]{:S(2)}, u32[]{:S(2)}) %collective-permute-start.24) | collective-permute-done | bytes 131104 | tf_op jit(solution)/shard_map/ppermute | solution.py:26
  131.4 3.3 %collective-permute-done.25.refs_14_ = f32[32,1024]{1,0:T(8,128)S(1)} collective-permute-done((f32[32,1024]{1,0:T(8,128)S(1)}, f32[32,1024]{1,0:T(8,128)S(1)}, u32[]{:S(2)}, u32[]{:S(2)}) %collective-permute-start.25) | collective-permute-done | bytes 131104 | tf_op jit(solution)/shard_map/ppermute | solution.py:26
  134.9 31.5 %all_to_all.10.refs_0_ = f32[16,16,1024]{2,1,0:T(8,128)S(1)} all-to-all(f32[16,16,1024]{2,1,0:T(8,128)S(1)} %shard_map.41), channel_id=1, replica_groups=mesh['zh'=4,'y'=4,'zl'=2,'c'=2,'x'=4] {'zh','y'}, dimensions={0} | all-to-all | bytes 2097152 | tf_op jit(solution)/shard_map/all_to_all | solution.py:296
  166.4 4.2 %all-to-all-start = ((f32[16,16,1024]{2,1,0:T(8,128)}), f32[16,16,1024]{2,1,0:T(8,128)S(1)}, u32[]{:S(2)}, u32[]{:S(2)}) async-start(f32[16,16,1024]{2,1,0:T(8,128)} %bitcast.7), calls=%async_computation.1 | async-start | bytes 2097152 | tf_op jit(solution)/shard_map/all_to_all | solution.py:296
  170.6 1.8 shard_map.42.refs_1_
  172.4 27.7 %all-to-all-done.refs_0_ = f32[16,16,1024]{2,1,0:T(8,128)S(1)} async-done(((f32[16,16,1024]{2,1,0:T(8,128)}), f32[16,16,1024]{2,1,0:T(8,128)S(1)}, u32[]{:S(2)}, u32[]{:S(2)}) %all-to-all-start) | async-done | bytes 1048608 | tf_op jit(solution)/shard_map/all_to_all | solution.py:296
  200.1 1.8 shard_map.43
  (59 shorter events, 14.6 us)
Async XLA Ops:
  6.5 159.9 %reduce-scatter.2.cloned.1.call-start = ((), (), s32[]{:S(2)}) async-start(), calls=%async_computation.3 | async-start | bytes 5242880 | tf_op jit(solution)/shard_map/reduce_scatter | solution.py:291
  8.2 15.3 %collective-permute-start = (f32[4,16,1024]{2,1,0:T(8,128)S(1)}, f32[4,16,1024]{2,1,0:T(8,128)S(1)}, u32[]{:S(2)}, u32[]{:S(2)}) collective-permute-start(f32[4,16,1024]{2,1,0:T(8,128)S(1)} %shard_map.28.refs_0_), channel_id=1, source_target_pairs={{0,192},{1,193},{2,194},{3,195},{4,196},{5,197},{6,198},{7,199},{8... | collective-permute-start | bytes 786440 | tf_op jit(solution)/shard_map/ppermute | solution.py:26
  13.6 15.5 %collective-permute-start.1 = (f32[4,16,1024]{2,1,0:T(8,128)S(1)}, f32[4,16,1024]{2,1,0:T(8,128)S(1)}, u32[]{:S(2)}, u32[]{:S(2)}) collective-permute-start(f32[4,16,1024]{2,1,0:T(8,128)S(1)} %shard_map.28.refs_0_), channel_id=1, source_target_pairs={{0,64},{1,65},{2,66},{3,67},{4,68},{5,69},{6,70},{7,71},{8,72},{9,... | collective-permute-start | bytes 786440 | tf_op jit(solution)/shard_map/ppermute | solution.py:26
  13.6 15.5 %collective-permute-start.2 = (f32[4,16,1024]{2,1,0:T(8,128)S(1)}, f32[4,16,1024]{2,1,0:T(8,128)S(1)}, u32[]{:S(2)}, u32[]{:S(2)}) collective-permute-start(f32[4,16,1024]{2,1,0:T(8,128)S(1)} %shard_map.28.refs_0_), channel_id=1, source_target_pairs={{0,16},{1,17},{2,18},{3,19},{4,20},{5,21},{6,22},{7,23},{8,24},{9,... | collective-permute-start | bytes 786440 | tf_op jit(solution)/shard_map/ppermute | solution.py:26
  15.2 13.9 %collective-permute-start.3 = (f32[4,16,1024]{2,1,0:T(8,128)S(1)}, f32[4,16,1024]{2,1,0:T(8,128)S(1)}, u32[]{:S(2)}, u32[]{:S(2)}) collective-permute-start(f32[4,16,1024]{2,1,0:T(8,128)S(1)} %shard_map.28.refs_0_), channel_id=1, source_target_pairs={{0,48},{1,49},{2,50},{3,51},{4,52},{5,53},{6,54},{7,55},{8,56},{9,... | collective-permute-start | bytes 786440 | tf_op jit(solution)/shard_map/ppermute | solution.py:26
  16.9 12.6 %collective-permute-start.4 = (f32[4,16,1024]{2,1,0:T(8,128)S(1)}, f32[4,16,1024]{2,1,0:T(8,128)S(1)}, u32[]{:S(2)}, u32[]{:S(2)}) collective-permute-start(f32[4,16,1024]{2,1,0:T(8,128)S(1)} %shard_map.28.refs_0_), channel_id=1, source_target_pairs={{0,32},{1,33},{2,34},{3,35},{4,36},{5,37},{6,38},{7,39},{8,40},{9,... | collective-permute-start | bytes 786440 | tf_op jit(solution)/shard_map/ppermute | solution.py:26
  29.5 8.9 %collective-permute-start.5 = (f32[512,1024]{1,0:T(8,128)}, f32[512,1024]{1,0:T(8,128)S(1)}, u32[]{:S(2)}, u32[]{:S(2)}) collective-permute-start(f32[512,1024]{1,0:T(8,128)} %value.1), channel_id=1, source_target_pairs={{0,4},{1,5},{2,6},{3,7},{4,0},{5,1},{6,2},{7,3},{8,12},{9,13},{10,... | collective-permute-start | bytes 6291464 | tf_op jit(solution)/shard_map/ppermute | solution.py:26
  29.5 21.6 %collective-permute-start.7 = (f32[2,4,16,1024]{3,2,1,0:T(8,128)S(1)}, f32[2,4,16,1024]{3,2,1,0:T(8,128)S(1)}, u32[]{:S(2)}, u32[]{:S(2)}) collective-permute-start(f32[2,4,16,1024]{3,2,1,0:T(8,128)S(1)} %shard_map.32.refs_0_), channel_id=1, source_target_pairs={{0,16},{1,17},{2,18},{3,19},{4,20},{5,21},{6,22},{7,23},{8,24},{9,... | collective-permute-start | bytes 1572872 | tf_op jit(solution)/shard_map/ppermute | solution.py:26
  30.9 20.1 %collective-permute-start.8 = (f32[2,4,16,1024]{3,2,1,0:T(8,128)S(1)}, f32[2,4,16,1024]{3,2,1,0:T(8,128)S(1)}, u32[]{:S(2)}, u32[]{:S(2)}) collective-permute-start(f32[2,4,16,1024]{3,2,1,0:T(8,128)S(1)} %shard_map.32.refs_0_), channel_id=1, source_target_pairs={{0,48},{1,49},{2,50},{3,51},{4,52},{5,53},{6,54},{7,55},{8,56},{9,... | collective-permute-start | bytes 1572872 | tf_op jit(solution)/shard_map/ppermute | solution.py:26
  34.8 16.3 %collective-permute-start.6 = (f32[4,16,1024]{2,1,0:T(8,128)S(1)}, f32[4,16,1024]{2,1,0:T(8,128)S(1)}, u32[]{:S(2)}, u32[]{:S(2)}) collective-permute-start(f32[4,16,1024]{2,1,0:T(8,128)S(1)} %shard_map.28.refs_0_), channel_id=1, source_target_pairs={{0,128},{1,129},{2,130},{3,131},{4,132},{5,133},{6,134},{7,135},{8... | collective-permute-start | bytes 786440 | tf_op jit(solution)/shard_map/ppermute | solution.py:26
  38.7 12.4 %copy-start.2 = (f32[512,1024]{1,0:T(8,128)S(1)}, f32[512,1024]{1,0:T(8,128)}, u32[]{:S(2)}) copy-start(f32[512,1024]{1,0:T(8,128)} %value.1) | copy-start | bytes 6291460
  41.3 9.8 %collective-permute-start.10 = (f32[64,1024]{1,0:T(8,128)S(1)}, f32[64,1024]{1,0:T(8,128)S(1)}, u32[]{:S(2)}, u32[]{:S(2)}) collective-permute-start(f32[64,1024]{1,0:T(8,128)S(1)} %get-tuple-element.78), channel_id=1, source_target_pairs={{0,3},{1,0},{2,1},{3,2},{4,7},{5,4},{6,5},{7,6},{8,11},{9,8},{10,9... | collective-permute-start | bytes 786440 | tf_op jit(solution)/shard_map/ppermute | solution.py:26
  42.2 8.9 %collective-permute-start.9 = (f32[64,1024]{1,0:T(8,128)S(1)}, f32[64,1024]{1,0:T(8,128)S(1)}, u32[]{:S(2)}, u32[]{:S(2)}) collective-permute-start(f32[64,1024]{1,0:T(8,128)S(1)} %get-tuple-element.77), channel_id=1, source_target_pairs={{0,1},{1,2},{2,3},{3,0},{4,5},{5,6},{6,7},{7,4},{8,9},{9,10},{10,1... | collective-permute-start | bytes 786440 | tf_op jit(solution)/shard_map/ppermute | solution.py:26
  51.1 26.6 %collective-permute-start.14 = (f32[512,1024]{1,0:T(8,128)S(1)}, f32[512,1024]{1,0:T(8,128)S(1)}, u32[]{:S(2)}, u32[]{:S(2)}) collective-permute-start(f32[512,1024]{1,0:T(8,128)S(1)} %copy-done.2), channel_id=1, source_target_pairs={{0,200},{1,201},{2,202},{3,203},{4,12},{5,13},{6,14},{7,15},{8,0},... | collective-permute-start | bytes 6291464 | tf_op jit(solution)/shard_map/ppermute | solution.py:26
  51.6 21.5 %collective-permute-start.11 = (f32[4,32,1024]{2,1,0:T(8,128)S(1)}, f32[4,32,1024]{2,1,0:T(8,128)S(1)}, u32[]{:S(2)}, u32[]{:S(2)}) collective-permute-start(f32[4,32,1024]{2,1,0:T(8,128)S(1)} %get-tuple-element.85), channel_id=1, source_target_pairs={{0,16},{1,17},{2,18},{3,19},{4,20},{5,21},{6,22},{7,23},{8,24},{9,... | collective-permute-start | bytes 1572872 | tf_op jit(solution)/shard_map/ppermute | solution.py:26
  51.6 21.4 %collective-permute-start.12 = (f32[4,32,1024]{2,1,0:T(8,128)S(1)}, f32[4,32,1024]{2,1,0:T(8,128)S(1)}, u32[]{:S(2)}, u32[]{:S(2)}) collective-permute-start(f32[4,32,1024]{2,1,0:T(8,128)S(1)} %get-tuple-element.86), channel_id=1, source_target_pairs={{0,48},{1,49},{2,50},{3,51},{4,52},{5,53},{6,54},{7,55},{8,56},{9,... | collective-permute-start | bytes 1572872 | tf_op jit(solution)/shard_map/ppermute | solution.py:26
  54.9 17.8 %collective-permute-start.13 = (f32[4,16,1024]{2,1,0:T(8,128)S(1)}, f32[4,16,1024]{2,1,0:T(8,128)S(1)}, u32[]{:S(2)}, u32[]{:S(2)}) collective-permute-start(f32[4,16,1024]{2,1,0:T(8,128)S(1)} %collective-permute-done.6.own.refs_0_), channel_id=1, source_target_pairs={{0,32},{1,33},{2,34},{3,35},{4,36},{5,37},{6,38},{7,39},{8,40},{9,... | collective-permute-start | bytes 786440 | tf_op jit(solution)/shard_map/ppermute | solution.py:26
  77.7 24.5 %collective-permute-start.15 = (f32[512,1024]{1,0:T(8,128)S(1)}, f32[512,1024]{1,0:T(8,128)S(1)}, u32[]{:S(2)}, u32[]{:S(2)}) collective-permute-start(f32[512,1024]{1,0:T(8,128)S(1)} %collective-permute-done.14.refs_8_), channel_id=1, source_target_pairs={{0,4},{1,5},{2,6},{3,7},{4,0},{5,1},{6,2},{7,3},{8,12},{9,13},{10,... | collective-permute-start | bytes 6291464 | tf_op jit(solution)/shard_map/ppermute | solution.py:26
  77.8 24.5 %collective-permute-start.18 = (f32[128,1024]{1,0:T(8,128)S(1)}, f32[128,1024]{1,0:T(8,128)S(1)}, u32[]{:S(2)}, u32[]{:S(2)}) collective-permute-start(f32[128,1024]{1,0:T(8,128)S(1)} %get-tuple-element.91), channel_id=1, source_target_pairs={{0,1},{1,2},{2,3},{3,0},{4,5},{5,6},{6,7},{7,4},{8,9},{9,10},{10,1... | collective-permute-start | bytes 1572872 | tf_op jit(solution)/shard_map/ppermute | solution.py:26
  79.7 22.6 %collective-permute-start.19 = (f32[128,1024]{1,0:T(8,128)S(1)}, f32[128,1024]{1,0:T(8,128)S(1)}, u32[]{:S(2)}, u32[]{:S(2)}) collective-permute-start(f32[128,1024]{1,0:T(8,128)S(1)} %get-tuple-element.92), channel_id=1, source_target_pairs={{0,3},{1,0},{2,1},{3,2},{4,7},{5,4},{6,5},{7,6},{8,11},{9,8},{10,9... | collective-permute-start | bytes 1572872 | tf_op jit(solution)/shard_map/ppermute | solution.py:26
  79.8 15.1 %collective-permute-start.16 = (f32[32,1024]{1,0:T(8,128)S(1)}, f32[32,1024]{1,0:T(8,128)S(1)}, u32[]{:S(2)}, u32[]{:S(2)}) collective-permute-start(f32[32,1024]{1,0:T(8,128)S(1)} %get-tuple-element.104), channel_id=1, source_target_pairs={{0,1},{1,2},{2,3},{3,0},{4,5},{5,6},{6,7},{7,4},{8,9},{9,10},{10,1... | collective-permute-start | bytes 393224 | tf_op jit(solution)/shard_map/ppermute | solution.py:26
  83.0 14.7 %collective-permute-start.17 = (f32[32,1024]{1,0:T(8,128)S(1)}, f32[32,1024]{1,0:T(8,128)S(1)}, u32[]{:S(2)}, u32[]{:S(2)}) collective-permute-start(f32[32,1024]{1,0:T(8,128)S(1)} %get-tuple-element.105), channel_id=1, source_target_pairs={{0,3},{1,0},{2,1},{3,2},{4,7},{5,4},{6,5},{7,6},{8,11},{9,8},{10,9... | collective-permute-start | bytes 393224 | tf_op jit(solution)/shard_map/ppermute | solution.py:26
  85.6 16.7 %copy-start.4 = (f32[32,1024]{1,0:T(8,128)}, f32[32,1024]{1,0:T(8,128)S(1)}, u32[]{:S(2)}) copy-start(f32[32,1024]{1,0:T(8,128)S(1)} %get-tuple-element.120.left_high) | copy-start | bytes 393220
  85.6 16.7 %copy-start.6 = (f32[64,1024]{1,0:T(8,128)}, f32[64,1024]{1,0:T(8,128)S(1)}, u32[]{:S(2)}) copy-start(f32[64,1024]{1,0:T(8,128)S(1)} %get-tuple-element.114) | copy-start | bytes 786436
  85.6 16.7 %copy-start.7 = (f32[64,1024]{1,0:T(8,128)}, f32[64,1024]{1,0:T(8,128)S(1)}, u32[]{:S(2)}) copy-start(f32[64,1024]{1,0:T(8,128)S(1)} %get-tuple-element.113) | copy-start | bytes 786436
  108.8 9.5 %collective-permute-start.22 = (f32[64,1024]{1,0:T(8,128)}, f32[64,1024]{1,0:T(8,128)S(1)}, u32[]{:S(2)}, u32[]{:S(2)}) collective-permute-start(f32[64,1024]{1,0:T(8,128)} %copy-done.7), channel_id=1, source_target_pairs={{0,1},{1,2},{2,3},{3,0},{4,5},{5,6},{6,7},{7,4},{8,9},{9,10},{10,1... | collective-permute-start | bytes 786440 | tf_op jit(solution)/shard_map/ppermute | solution.py:26
  109.2 10.7 %collective-permute-start.23 = (f32[64,1024]{1,0:T(8,128)}, f32[64,1024]{1,0:T(8,128)S(1)}, u32[]{:S(2)}, u32[]{:S(2)}) collective-permute-start(f32[64,1024]{1,0:T(8,128)} %copy-done.6), channel_id=1, source_target_pairs={{0,3},{1,0},{2,1},{3,2},{4,7},{5,4},{6,5},{7,6},{8,11},{9,8},{10,9... | collective-permute-start | bytes 786440 | tf_op jit(solution)/shard_map/ppermute | solution.py:26
  111.0 23.7 %collective-permute-start.20 = (f32[64,1024]{1,0:T(8,128)S(1)}, f32[64,1024]{1,0:T(8,128)S(1)}, u32[]{:S(2)}, u32[]{:S(2)}) collective-permute-start(f32[64,1024]{1,0:T(8,128)S(1)} %get-tuple-element.111), channel_id=1, source_target_pairs={{0,1},{1,2},{2,3},{3,0},{4,5},{5,6},{6,7},{7,4},{8,9},{9,10},{10,1... | collective-permute-start | bytes 786440 | tf_op jit(solution)/shard_map/ppermute | solution.py:26
  112.5 22.2 %collective-permute-start.21 = (f32[64,1024]{1,0:T(8,128)S(1)}, f32[64,1024]{1,0:T(8,128)S(1)}, u32[]{:S(2)}, u32[]{:S(2)}) collective-permute-start(f32[64,1024]{1,0:T(8,128)S(1)} %get-tuple-element.112), channel_id=1, source_target_pairs={{0,3},{1,0},{2,1},{3,2},{4,7},{5,4},{6,5},{7,6},{8,11},{9,8},{10,9... | collective-permute-start | bytes 786440 | tf_op jit(solution)/shard_map/ppermute | solution.py:26
  120.8 10.6 %collective-permute-start.24 = (f32[32,1024]{1,0:T(8,128)S(1)}, f32[32,1024]{1,0:T(8,128)S(1)}, u32[]{:S(2)}, u32[]{:S(2)}) collective-permute-start(f32[32,1024]{1,0:T(8,128)S(1)} %get-tuple-element.121), channel_id=1, source_target_pairs={{0,1},{1,2},{2,3},{3,0},{4,5},{5,6},{6,7},{7,4},{8,9},{9,10},{10,1... | collective-permute-start | bytes 393224 | tf_op jit(solution)/shard_map/ppermute | solution.py:26
  120.9 13.8 %collective-permute-start.25 = (f32[32,1024]{1,0:T(8,128)S(1)}, f32[32,1024]{1,0:T(8,128)S(1)}, u32[]{:S(2)}, u32[]{:S(2)}) collective-permute-start(f32[32,1024]{1,0:T(8,128)S(1)} %get-tuple-element.122), channel_id=1, source_target_pairs={{0,3},{1,0},{2,1},{3,2},{4,7},{5,4},{6,5},{7,6},{8,11},{9,8},{10,9... | collective-permute-start | bytes 393224 | tf_op jit(solution)/shard_map/ppermute | solution.py:26
  166.4 33.7 %all-to-all-start = ((f32[16,16,1024]{2,1,0:T(8,128)}), f32[16,16,1024]{2,1,0:T(8,128)S(1)}, u32[]{:S(2)}, u32[]{:S(2)}) async-start(f32[16,16,1024]{2,1,0:T(8,128)} %bitcast.7), calls=%async_computation.1 | async-start | bytes 2097152 | tf_op jit(solution)/shard_map/all_to_all | solution.py:296
  (4 other events, 5.4 us)
Sparse Core Ops, SparseCore 0:
  108.9 52.7 reduce-scatter.1
